TPU v7x, 32 devices: a whole 2x2x4 slice. The times are simulated.
32 devices in a mesh: expert: 4 (over y, x), req: 8 (over z, core).
Axes of the slice: x: 2, y: 2, z: 4, core: 2. Of those that a mesh axis runs over, the one named last changes fastest.
Arguments:
- queries: bfloat16 [8192, 1024], P(('expert', 'req')), may hold values from -82 to 82
- self_kv: bfloat16 [8192, 2048], P(('expert', 'req')), may hold values from -4 to 4
- kv_pages: bfloat16 [32, 128, 2048], P(('expert', 'req')), may hold values from -4 to 4
- page_table: int32 [4, 8], P('expert'), may hold values from 0 to 7, as said below
- lengths: int32 [8192], P(('expert', 'req')), may hold values from 1 to 1024
- routes: int32 [8192, 2], P(('expert', 'req')), may hold values from 0 to 3, all different within a row
- residual: bfloat16 [8192, 1024], P(('expert', 'req')), may hold values from -20 to 20
- w_attn_out: bfloat16 [1024, 1024], replicated, may hold values from -0.1875 to 0.1875
- gain_attn: bfloat16 [1024], replicated, may hold values from 0.25 to 1.75
- w_router: bfloat16 [1024, 4], replicated, may hold values from -0.1875 to 0.1875
- w_in: bfloat16 [4, 1024, 2816], P('expert'), may hold values from -0.1875 to 0.1875
- w_out: bfloat16 [4, 1408, 1024], P('expert'), may hold values from -0.15625 to 0.15625
- gain_out: bfloat16 [1024], replicated, may hold values from 0.25 to 1.75
Outputs:
- layer_out: bfloat16 [8192, 1024], P(('expert', 'req'))
Inputs may be any that keep to these rules, and one draw needn't show every extreme that they name: Each row of page_table is a permutation of 0 to 7.
All inputs are finite; a program needn't handle non-finite values.
Results may differ from a plain program's by a relative error of at most 0.01.
Values may be sent and summed in bfloat16 or wider, within the bound.
A program may use at most 128 MiB of HBM per device.

v0:
```python
import math

import jax
import jax.numpy as jnp
from jax import lax
from jax.sharding import PartitionSpec as P

HEADS = 16
HEAD_DIM = 64
TOP = 2
PAGE = 128
HD = 1024


norm_eps = 1e-06


def block_size(total_count, largest):
    chosen = min(total_count, largest)
    while total_count % chosen:
        chosen -= 1
    return chosen


def key_positions(table_row, key_count, page_len):
    logical = jnp.arange(table_row.shape[0], dtype=jnp.int32)
    inverse = jnp.sum(
        jnp.where(table_row[:, None] == logical[None, :], logical[:, None], 0), axis=0
    )
    flat_index = jnp.arange(key_count, dtype=jnp.int32)
    page_index = flat_index // page_len
    logical_page = jnp.sum(
        jnp.where(page_index[:, None] == logical[None, :], inverse[None, :], 0), axis=1
    )
    return logical_page * page_len + flat_index % page_len


def rms_scale(values, gain_row):
    mean_square = jnp.mean(values * values, axis=-1, keepdims=True)
    return values * lax.rsqrt(mean_square + norm_eps) * gain_row.astype(jnp.float32)


def route_block(route_rows, cap_size, expert_count):
    onehot = (
        route_rows[:, :, None] == jnp.arange(expert_count, dtype=jnp.int32)[None, None, :]
    ).astype(jnp.int32)
    ordered = onehot.transpose(1, 0, 2).reshape(-1, expert_count)
    earlier = jnp.cumsum(ordered, axis=0) - ordered
    position = jnp.sum(earlier * ordered, axis=1).reshape(route_rows.shape[1], route_rows.shape[0])
    kept_mask = position < cap_size
    slot_ids = jnp.where(kept_mask, route_rows.T * cap_size + position, -1)
    return (onehot, kept_mask, slot_ids)


def on_device(
    queries,
    self_kv,
    kv_pages,
    page_table,
    lengths,
    routes,
    residual,
    w_attn_out,
    gain_attn,
    w_router,
    w_in,
    w_out,
    gain_out,
):
    row_count = queries.shape[0]
    scale_qk = 1.0 / math.sqrt(HEAD_DIM)
    table_row = page_table[0]
    page_rows = kv_pages.reshape(-1, kv_pages.shape[-1])
    query_h = queries.reshape(row_count, HEADS, HEAD_DIM)
    own_key = self_kv[:, :HD].reshape(row_count, HEADS, HEAD_DIM)
    own_value = self_kv[:, HD:].reshape(row_count, HEADS, HEAD_DIM)
    own_score = (
        jnp.einsum("rhd,rhd->hr", query_h, own_key, preferred_element_type=jnp.float32) * scale_qk
    )
    start_value = jnp.swapaxes(own_value, 0, 1).astype(jnp.float32)
    initial = (own_score, jnp.ones_like(own_score), start_value)
    page_piece = lax.all_gather(page_rows, "req", axis=0, tiled=True)
    piece_len = page_piece.shape[0]
    step_len = block_size(piece_len, 512)
    positions = key_positions(table_row, piece_len, PAGE)
    blocks = page_piece.reshape(piece_len // step_len, step_len, page_piece.shape[1])
    block_pos = positions.reshape(piece_len // step_len, step_len)

    def add_block(running, block_items):
        highest, weight_sum, weighted = running
        block_rows, block_place = block_items
        key_rows = block_rows[:, :HD].reshape(step_len, HEADS, HEAD_DIM)
        value_rows = block_rows[:, HD:].reshape(step_len, HEADS, HEAD_DIM)
        scores = (
            jnp.einsum("rhd,khd->hrk", query_h, key_rows, preferred_element_type=jnp.float32)
            * scale_qk
        )
        visible = block_place[None, :] < lengths[:, None]
        masked = jnp.where(visible[None], scores, -jnp.inf)
        new_high = jnp.maximum(highest, jnp.max(masked, axis=2))
        factor = jnp.exp(highest - new_high)
        weights = jnp.exp(masked - new_high[:, :, None])
        weight_sum = weight_sum * factor + jnp.sum(weights, axis=2)
        weighted = weighted * factor[:, :, None] + jnp.einsum(
            "hrk,khd->hrd",
            weights.astype(jnp.bfloat16),
            value_rows,
            preferred_element_type=jnp.float32,
        )
        return ((new_high, weight_sum, weighted), None)

    result, unused = lax.scan(add_block, initial, (blocks, block_pos))
    highest, weight_sum, weighted = result
    attended = (
        (weighted / weight_sum[:, :, None])
        .transpose(1, 0, 2)
        .reshape(row_count, HD)
        .astype(jnp.bfloat16)
    )
    residual_sum = residual.astype(jnp.float32) + jnp.dot(
        attended, w_attn_out, preferred_element_type=jnp.float32
    )
    normed = rms_scale(residual_sum, gain_attn).astype(jnp.bfloat16)
    logits = jnp.dot(normed, w_router, preferred_element_type=jnp.float32)
    experts_all = w_router.shape[1]
    cap_size = (5 * row_count * TOP + 4 * experts_all - 1) // (4 * experts_all)
    onehot, kept_mask, slot_ids = route_block(routes, cap_size, experts_all)
    picked = jnp.sum(jnp.where(onehot > 0, logits[:, None, :], 0.0), axis=2)
    gate_values = jax.nn.sigmoid(picked - picked[:, ::-1])
    slot_range = jnp.arange(experts_all * cap_size, dtype=jnp.int32)
    assign = jnp.sum(
        (slot_ids[:, None, :] == slot_range[None, :, None]).astype(jnp.bfloat16), axis=0
    )
    model_width = normed.shape[1]
    buffer = (
        jnp.dot(assign, normed, preferred_element_type=jnp.float32)
        .astype(jnp.bfloat16)
        .reshape(experts_all, cap_size, model_width)
    )
    arrived = lax.all_to_all(buffer, "expert", split_axis=0, concat_axis=0, tiled=True)
    slot_count = arrived.shape[1]
    local_experts = w_in.shape[0]
    hidden_width = w_out.shape[1]
    grouped = arrived.reshape(-1, local_experts, slot_count, model_width)
    inner_act = jnp.einsum("slnd,ldf->slnf", grouped, w_in, preferred_element_type=jnp.float32)
    hidden = (
        jax.nn.gelu(inner_act[..., :hidden_width], approximate=True) * inner_act[..., hidden_width:]
    ).astype(jnp.bfloat16)
    outcome = jnp.einsum(
        "slnf,lfd->slnd", hidden, w_out, preferred_element_type=jnp.float32
    ).astype(jnp.bfloat16)
    expert_done = outcome.reshape(-1, slot_count, model_width)
    collected = lax.all_to_all(expert_done, "expert", split_axis=0, concat_axis=0, tiled=True)
    flat_rows = collected.reshape(-1, model_width)
    picked_rows = flat_rows[jnp.maximum(slot_ids, 0)]
    gate_kept = jnp.where(kept_mask, gate_values.T, 0.0)
    mixture = jnp.sum(picked_rows.astype(jnp.float32) * gate_kept[:, :, None], axis=0)
    return rms_scale(residual_sum + mixture, gain_out).astype(jnp.bfloat16)


def solution(mesh):
    in_specs = (
        P(("expert", "req"), None),
        P(("expert", "req"), None),
        P(("expert", "req"), None, None),
        P("expert", None),
        P(("expert", "req")),
        P(("expert", "req"), None),
        P(("expert", "req"), None),
        P(),
        P(),
        P(),
        P("expert", None, None),
        P("expert", None, None),
        P(),
    )
    out_specs = P(("expert", "req"), None)
    return jax.shard_map(
        on_device, mesh=mesh, in_specs=in_specs, out_specs=out_specs, check_vma=False
    )
```

profile of v0, /device:TPU:0, one launch (start us, length us, event | category | flops | bytes accessed | tf_op | source)
XLA Modules:
  0.0 183.3 jit_solution(17256257046171117510)
XLA Ops:
  7.3 2.5 %slice_convert_fusion = (f32[256,1024]{1,0:T(8,128)}, bf16[256,1024]{1,0:T(8,128)(2,1)S(1)}) fusion(bf16[256,2048]{1,0:T(8,128)(2,1)} %param.16), kind=kLoop, calls=%fused_computation.51 | loop fusion | flops 262144 | bytes 2621440 | tf_op jit(solution)/shard_map/convert_element_type | solution.py:80
  12.0 2.6 %copy.29 = f32[256,1024]{0,1:T(8,128)} copy(f32[256,1024]{1,0:T(8,128)} %get-tuple-element.119) | data formatting | bytes 2097152 | tf_op jit(solution)/shard_map/convert_element_type | solution.py:80
  18.7 1.2 fusion.40
  21.2 37.7 %all-gather.3.cloned.1.call-done = bf16[1,1024,2048]{2,1,0:T(8,128)(2,1)} async-done(((bf16[1,128,2048]{2,1,0:T(8,128)(2,1)}), bf16[1,1024,2048]{2,1,0:T(8,128)(2,1)}) %all-gather.3.cloned.1.call-update) | async-done | bytes 4194320 | tf_op jit(solution)/shard_map/all_gather | solution.py:82
  58.9 54.3 %while.15 = (s32[]{:T(128)}, f32[16,256]{1,0:T(8,128)}, f32[16,256]{1,0:T(8,128)}, f32[16,256,64]{1,2,0:T(8,128)}, s32[2,512]{1,0:T(2,128)}, /*index=5*/s32[256]...) while((s32[]{:T(128)}, f32[16,256]{1,0:T(8,128)}, ...), condition=%wide.region_5.6_spmd.clone, body=%wide.region_2.5_spmd.clone.sunk | while | flops 560607232 | bytes 76881064 | solution.py:112
  60.4 3.1 %constant_dynamic-slice_fusion.5 = bf16[1,512,2048]{2,1,0:T(8,128)(2,1)} fusion(bf16[2,512,2048]{2,1,0:T(8,128)(2,1)} %get-tuple-element.210, s32[]{:T(128)} %get-tuple-element.194), kind=kLoop, calls=%fused_computation.13.clone.1 | loop fusion | bytes 4194308 | tf_op jit(solution)/shard_map/while/body/jit(dynamic_index_in_dim)/dynamic_slice | solution.py:112
  63.5 3.9 %copy.48 = bf16[1,512,2048]{1,2,0:T(8,128)(2,1)} copy(bf16[1,512,2048]{2,1,0:T(8,128)(2,1)} %constant_dynamic-slice_fusion.5) | data formatting | bytes 4194304 | tf_op jit(solution)/shard_map/while/body/jit(dynamic_index_in_dim)/dynamic_slice | solution.py:112
  67.4 2.6 %fusion.78 = (bf16[512,1024]{0,1:T(8,128)(2,1)}, bf16[512,1024]{0,1:T(8,128)(2,1)S(1)}) fusion(bf16[512,2048]{0,1:T(8,128)(2,1)} %bitcast.117), kind=kLoop, calls=%fused_computation.94.clone.1 | loop fusion | bytes 4194304 | tf_op jit(solution)/shard_map/while/body/eval_jaxpr/slice | solution.py:93
  70.1 1.5 fusion.79
  71.6 3.2 %copy-done.1 = f32[16,512,256]{2,1,0:T(8,128)} copy-done((f32[16,512,256]{2,1,0:T(8,128)}, f32[16,512,256]{2,1,0:T(8,128)S(1)}, u32[]{:S(2)}) %copy-start.1) | copy-done | bytes 8388632 | tf_op jit(solution)/shard_map/while
  74.8 2.3 %fusion.80 = f32[16,256]{1,0:T(8,128)} fusion(f32[16,512,256]{2,1,0:T(8,128)S(1)} %get-tuple-element.180, f32[16,256]{1,0:T(8,128)S(1)} %max.10, pred[256,512]{0,1:T(8,128)(4,1)S(1)} %broadcast_compare_fusion.3), kind=kLoop, calls=%fused_computation.4.clone.1 | loop fusion | flops 8384512 | bytes 8552448 | tf_op jit(solution)/shard_map/while/body/eval_jaxpr/reduce_sum | solution.py:103
  77.1 1.3 fusion.81
  78.4 7.0 %fusion.82 = f32[16,256,64]{1,2,0:T(8,128)} fusion(bf16[512,16,64]{0,2,1:T(8,128)(2,1)} %bitcast.120, f32[16,512,256]{2,1,0:T(8,128)} %copy-done.1, f32[16,256]{1,0:T(8,128)S(1)} %max.10, pred[256,512]{0,1:T(8,128)(4,1)S(1)} %broadcast_compare_fusion.3, f32[16,256,64]{1,2,0:T(8,128)} %get-tuple-element.197, f32[16,256]{1,0:T(8,128)S(1)} %get-tuple-element.183), kind=kOutput, calls=%fused_computation.8.clone.1 | convolution fusion | flops 277348352 | bytes 11698176 | tf_op jit(solution)/shard_map/while/body/eval_jaxpr/hrk,khd->hrd/dot_general | solution.py:104
  87.5 3.1 %constant_dynamic-slice_fusion.5 = bf16[1,512,2048]{2,1,0:T(8,128)(2,1)} fusion(bf16[2,512,2048]{2,1,0:T(8,128)(2,1)} %get-tuple-element.210, s32[]{:T(128)} %get-tuple-element.194), kind=kLoop, calls=%fused_computation.13.clone.1 | loop fusion | bytes 4194308 | tf_op jit(solution)/shard_map/while/body/jit(dynamic_index_in_dim)/dynamic_slice | solution.py:112
  90.7 3.9 %copy.48 = bf16[1,512,2048]{1,2,0:T(8,128)(2,1)} copy(bf16[1,512,2048]{2,1,0:T(8,128)(2,1)} %constant_dynamic-slice_fusion.5) | data formatting | bytes 4194304 | tf_op jit(solution)/shard_map/while/body/jit(dynamic_index_in_dim)/dynamic_slice | solution.py:112
  94.6 2.6 %fusion.78 = (bf16[512,1024]{0,1:T(8,128)(2,1)}, bf16[512,1024]{0,1:T(8,128)(2,1)S(1)}) fusion(bf16[512,2048]{0,1:T(8,128)(2,1)} %bitcast.117), kind=kLoop, calls=%fused_computation.94.clone.1 | loop fusion | bytes 4194304 | tf_op jit(solution)/shard_map/while/body/eval_jaxpr/slice | solution.py:93
  97.2 1.5 fusion.79
  98.8 3.2 %copy-done.1 = f32[16,512,256]{2,1,0:T(8,128)} copy-done((f32[16,512,256]{2,1,0:T(8,128)}, f32[16,512,256]{2,1,0:T(8,128)S(1)}, u32[]{:S(2)}) %copy-start.1) | copy-done | bytes 8388632 | tf_op jit(solution)/shard_map/while
  102.0 2.3 %fusion.80 = f32[16,256]{1,0:T(8,128)} fusion(f32[16,512,256]{2,1,0:T(8,128)S(1)} %get-tuple-element.180, f32[16,256]{1,0:T(8,128)S(1)} %max.10, pred[256,512]{0,1:T(8,128)(4,1)S(1)} %broadcast_compare_fusion.3), kind=kLoop, calls=%fused_computation.4.clone.1 | loop fusion | flops 8384512 | bytes 8552448 | tf_op jit(solution)/shard_map/while/body/eval_jaxpr/reduce_sum | solution.py:103
  104.2 1.4 fusion.81
  105.6 7.0 %fusion.82 = f32[16,256,64]{1,2,0:T(8,128)} fusion(bf16[512,16,64]{0,2,1:T(8,128)(2,1)} %bitcast.120, f32[16,512,256]{2,1,0:T(8,128)} %copy-done.1, f32[16,256]{1,0:T(8,128)S(1)} %max.10, pred[256,512]{0,1:T(8,128)(4,1)S(1)} %broadcast_compare_fusion.3, f32[16,256,64]{1,2,0:T(8,128)} %get-tuple-element.197, f32[16,256]{1,0:T(8,128)S(1)} %get-tuple-element.183), kind=kOutput, calls=%fused_computation.8.clone.1 | convolution fusion | flops 277348352 | bytes 11698176 | tf_op jit(solution)/shard_map/while/body/eval_jaxpr/hrk,khd->hrd/dot_general | solution.py:104
  113.2 1.5 divide_convert_fusion
  114.7 2.7 %multiply_reduce_fusion.1 = (f32[256]{0:T(256)S(1)}, f32[256,1024]{1,0:T(8,128)S(1)}) fusion(bf16[256,1024]{0,1:T(8,128)(2,1)S(1)} %bitcast.125, bf16[1024,1024]{1,0:T(8,128)(2,1)} %param.22, bf16[256,1024]{1,0:T(8,128)(2,1)} %param.21), kind=kOutput, calls=%fused_computation.48 | convolution fusion | flops 537919232 | bytes 4195328 | tf_op jit(solution)/shard_map/dot_general | solution.py:120
  119.0 20.8 %all_to_all.10 = bf16[4,160,1024]{2,1,0:T(8,128)(2,1)S(1)} all-to-all(bf16[4,160,1024]{2,1,0:T(8,128)(2,1)S(1)} %bitcast.122), channel_id=1, replica_groups=mesh['expert'=4,'req'=8] {'expert'}, dimensions={0} | all-to-all | bytes 2621440 | tf_op jit(solution)/shard_map/all_to_all | solution.py:140
  139.8 3.9 %fusion.14 = f32[4,1,160,2816]{3,2,0,1:T(8,128)S(1)} fusion(bf16[4,160,1024]{2,1,0:T(8,128)(2,1)S(1)} %all_to_all.10, bf16[1,1024,2816]{2,1,0:T(8,128)(2,1)S(1)} %bitcast.133), kind=kOutput, calls=%fused_computation.20 | convolution fusion | flops 3690987520 | bytes 14286848 | tf_op jit(solution)/shard_map/slnd,ldf->slnf/dot_general | solution.py:145
  143.7 3.6 %fusion.34 = bf16[4,160,1024]{2,1,0:T(8,128)(2,1)} fusion(bf16[1,1408,1024]{2,1,0:T(8,128)(2,1)S(1)} %copy-done, f32[4,1,160,2816]{3,2,0,1:T(8,128)S(1)} %fusion.14), kind=kOutput, calls=%fused_computation.39 | convolution fusion | flops 1855160320 | bytes 11403264 | tf_op jit(solution)/shard_map/slnf,lfd->slnd/dot_general | solution.py:149
  147.4 4.4 %all-to-all-start.1 = ((bf16[4,160,1024]{2,1,0:T(8,128)(2,1)}), bf16[4,160,1024]{2,1,0:T(8,128)(2,1)}, u32[]{:S(2)}, u32[]{:S(2)}) async-start(bf16[4,160,1024]{2,1,0:T(8,128)(2,1)} %fusion.34), calls=%async_computation.1 | async-start | bytes 2621440 | tf_op jit(solution)/shard_map/all_to_all | solution.py:153
  151.9 1.5 fusion.55
  153.6 13.9 %all-to-all-done.1 = bf16[4,160,1024]{2,1,0:T(8,128)(2,1)} async-done(((bf16[4,160,1024]{2,1,0:T(8,128)(2,1)}), bf16[4,160,1024]{2,1,0:T(8,128)(2,1)}, u32[]{:S(2)}, u32[]{:S(2)}) %all-to-all-start.1) | async-done | bytes 1310752 | tf_op jit(solution)/shard_map/all_to_all | solution.py:153
  167.5 5.0 %gather_fusion = bf16[512,1024]{1,0:T(8,128)(2,1)} fusion(bf16[640,1024]{1,0:T(8,128)(2,1)} %bitcast.26, s32[1024]{0:T(1024)S(1)} %pad_clamp_fusion), kind=kCustom, calls=%fused_computation | custom fusion | bytes 2099200 | tf_op jit(solution)/shard_map/gather | solution.py:155
  172.5 1.6 fusion.28
  174.1 1.4 multiply_reduce_fusion
  (79 shorter events, 15.2 us)
Async XLA Ops:
  6.5 137.2 %copy-start = (bf16[1,1408,1024]{2,1,0:T(8,128)(2,1)S(1)}, bf16[1,1408,1024]{2,1,0:T(8,128)(2,1)}, u32[]{:S(2)}) copy-start(bf16[1,1408,1024]{2,1,0:T(8,128)(2,1)} %param.26) | copy-start | bytes 8650756
  6.5 8.1 %copy-start.14 = (s32[1,8]{1,0:T(1,128)S(1)}, s32[1,8]{1,0:T(1,128)}, u32[]{:S(2)}) copy-start(s32[1,8]{1,0:T(1,128)} %param.18) | copy-start | bytes 100
  6.5 8.3 %copy-start.12 = (bf16[1024]{0:T(1024)(128)(2,1)S(1)}, bf16[1024]{0:T(1024)(128)(2,1)}, u32[]{:S(2)}) copy-start(bf16[1024]{0:T(1024)(128)(2,1)} %param.23) | copy-start | bytes 6148
  6.5 8.8 %copy-start.6 = (s32[256,2]{0,1:T(2,128)S(1)}, s32[256,2]{0,1:T(2,128)}, u32[]{:S(2)}) copy-start(s32[256,2]{0,1:T(2,128)} %param.20) | copy-start | bytes 6148
  6.5 52.3 %all-gather.3.cloned.1.call-start = ((), (), s32[]{:S(2)}) async-start(), calls=%async_computation.2 | async-start | bytes 4718592 | tf_op jit(solution)/shard_map/all_gather | solution.py:82
  17.1 41.7 %copy-start.8 = (s32[2,256]{1,0:T(2,128)}, s32[2,256]{1,0:T(2,128)S(1)}, u32[]{:S(2)}) copy-start(s32[2,256]{1,0:T(2,128)S(1)} %reshape.142) | copy-start | bytes 6148
  70.1 1.5 copy-start.3
  71.6 3.2 %copy-start.1 = (f32[16,512,256]{2,1,0:T(8,128)}, f32[16,512,256]{2,1,0:T(8,128)S(1)}, u32[]{:S(2)}) copy-start(f32[16,512,256]{2,1,0:T(8,128)S(1)} %get-tuple-element.180) | copy-start | bytes 25165828 | tf_op jit(solution)/shard_map/while
  97.2 1.5 copy-start.3
  98.7 3.2 %copy-start.1 = (f32[16,512,256]{2,1,0:T(8,128)}, f32[16,512,256]{2,1,0:T(8,128)S(1)}, u32[]{:S(2)}) copy-start(f32[16,512,256]{2,1,0:T(8,128)S(1)} %get-tuple-element.180) | copy-start | bytes 25165828 | tf_op jit(solution)/shard_map/while
  113.2 5.2 %copy-start.4 = (bf16[640,256]{1,0:T(8,128)(2,1)S(1)}, bf16[640,256]{1,0:T(8,128)(2,1)}, u32[]{:S(2)}) copy-start(bf16[640,256]{1,0:T(8,128)(2,1)} %fusion.41) | copy-start | bytes 983044
  113.2 5.2 %copy-start.5 = (f32[1024]{0:T(1024)S(1)}, f32[1024]{0:T(1024)}, u32[]{:S(2)}) copy-start(f32[1024]{0:T(1024)} %convert_element_type.77) | copy-start | bytes 12292
  113.2 26.6 %slice-start = ((s8[5767168]{0:T(1024)(128)(4,1)}), s8[4194304]{0:T(1024)(128)(4,1)S(1)}, s32[]{:S(2)}) async-start(s8[5767168]{0:T(1024)(128)(4,1)} %bitcast.132), calls=%async_computation.3 | async-start | bytes 8388608
  114.7 25.1 %slice-start.1 = ((s8[5767168]{0:T(1024)(128)(4,1)}), s8[1572864]{0:T(1024)(128)(4,1)S(1)}, s32[]{:S(2)}) async-start(s8[5767168]{0:T(1024)(128)(4,1)} %bitcast.132), calls=%async_computation.4 | async-start | bytes 3145728
  117.4 1.0 copy-start.2
  143.7 8.1 %copy-start.11 = (s32[1,2,2,128]{3,2,1,0:T(2,128)S(1)}, s32[1,2,2,128]{3,2,1,0:T(2,128)}, u32[]{:S(2)}) copy-start(s32[1,2,2,128]{3,2,1,0:T(2,128)} %get-tuple-element.113) | copy-start | bytes 6148
  143.7 8.1 %copy-start.13 = (bf16[1024]{0:T(1024)(128)(2,1)S(1)}, bf16[1024]{0:T(1024)(128)(2,1)}, u32[]{:S(2)}) copy-start(bf16[1024]{0:T(1024)(128)(2,1)} %param.27) | copy-start | bytes 6148
  143.7 8.1 %copy-start.10 = (bf16[1024,4]{0,1:T(4,128)(2,1)S(1)}, bf16[1024,4]{0,1:T(4,128)(2,1)}, u32[]{:S(2)}) copy-start(bf16[1024,4]{0,1:T(4,128)(2,1)} %param.24) | copy-start | bytes 24580
  147.4 6.0 %copy-start.7 = (s32[256,2]{0,1:T(2,128)S(1)}, s32[256,2]{0,1:T(2,128)}, u32[]{:S(2)}) copy-start(s32[256,2]{0,1:T(2,128)} %param.20) | copy-start | bytes 6148
  147.4 6.1 %copy-start.9 = (s32[2,256]{1,0:T(2,128)S(1)}, s32[2,256]{1,0:T(2,128)}, u32[]{:S(2)}) copy-start(s32[2,256]{1,0:T(2,128)} %copy-done.8) | copy-start | bytes 6148
  147.4 20.1 %all-to-all-start.1 = ((bf16[4,160,1024]{2,1,0:T(8,128)(2,1)}), bf16[4,160,1024]{2,1,0:T(8,128)(2,1)}, u32[]{:S(2)}, u32[]{:S(2)}) async-start(bf16[4,160,1024]{2,1,0:T(8,128)(2,1)} %fusion.34), calls=%async_computation.1 | async-start | bytes 2621440 | tf_op jit(solution)/shard_map/all_to_all | solution.py:153
Sparse Core Ops, SparseCore 0:
  9.0 49.8 all-gather.2
where the time goes:
time: 184 us; the launch traced here: 183 us
  waiting for transfers between devices  52.3 us (28%)
  local copies, waits for them, and re-layouts  39.6 us (22%)
  matrix products  29.3 us (16%)
  other arithmetic  23.2 us (13%)
  blocking collectives  20.8 us (11%)
  between operations  13.6 us (7%)
  starting transfers between devices  4.44 us (2%)
    all_gather x1, waiting for transfers between devices, on_device(): page_piece = lax.all_gather(page_rows, 'req', axis=0, tiled=True)  37.7 us
    all_to_all x1, blocking collectives, on_device(): lax.all_to_all(buffer, 'expert', split_axis=0, concat_axis=0, tiled=True)  20.8 us
    dynamic_slice x6, local copies, waits for them, and re-layouts, on_device(): result, unused = lax.scan(add_block, initial, (blocks, block_pos))  15.5 us
    dot_general x2, matrix products, add_block(): jnp.einsum('hrk,khd->hrd', weights.astype(jnp.bfloat16), value_rows, pref...  14 us
    all_to_all x1, waiting for transfers between devices, on_device(): lax.all_to_all(expert_done, 'expert', split_axis=0, concat_axis=0, tiled=...  13.9 us
    while x10, local copies, waits for them, and re-layouts  7.6 us
    slice x2, local copies, waits for them, and re-layouts, add_block(): value_rows = block_rows[:, HD:].reshape(step_len, HEADS, HEAD_DIM)  5.29 us
    gather x1, local copies, waits for them, and re-layouts, on_device(): picked_rows = flat_rows[jnp.maximum(slot_ids, 0)]  4.97 us
  transfers between devices with their start and end apart: 2, of which 2 were waited for; matrix products, arithmetic and copies ran while one was open for 8% of the time, Pallas kernels for 0%

commit v1 on v0

--- a/solution.py
+++ b/solution.py
@@ -45,7 +45,13 @@
         route_rows[:, :, None] == jnp.arange(expert_count, dtype=jnp.int32)[None, None, :]
     ).astype(jnp.int32)
     ordered = onehot.transpose(1, 0, 2).reshape(-1, expert_count)
-    earlier = jnp.cumsum(ordered, axis=0) - ordered
+    total = ordered.shape[0]
+    before = jnp.arange(total)[:, None] > jnp.arange(total)[None, :]
+    earlier = jnp.dot(
+        before.astype(jnp.bfloat16),
+        ordered.astype(jnp.bfloat16),
+        preferred_element_type=jnp.float32,
+    ).astype(jnp.int32)
     position = jnp.sum(earlier * ordered, axis=1).reshape(route_rows.shape[1], route_rows.shape[0])
     kept_mask = position < cap_size
     slot_ids = jnp.where(kept_mask, route_rows.T * cap_size + position, -1)

time: 184 us -> 184 us (level)
  no operation moved by 1% of the time
where the time goes in v1:
time: 184 us; the launch traced here: 183 us
  waiting for transfers between devices  53.7 us (29%)
  local copies, waits for them, and re-layouts  39.4 us (21%)
  matrix products  29.6 us (16%)
  other arithmetic  21.7 us (12%)
  blocking collectives  20.6 us (11%)
  between operations  13.6 us (7%)
  starting transfers between devices  4.44 us (2%)
    all_gather x1, waiting for transfers between devices, on_device(): page_piece = lax.all_gather(page_rows, 'req', axis=0, tiled=True)  39.1 us
    all_to_all x1, blocking collectives, on_device(): lax.all_to_all(buffer, 'expert', split_axis=0, concat_axis=0, tiled=True)  20.6 us
    dynamic_slice x6, local copies, waits for them, and re-layouts, on_device(): result, unused = lax.scan(add_block, initial, (blocks, block_pos))  15.5 us
    dot_general x2, matrix products, add_block(): jnp.einsum('hrk,khd->hrd', weights.astype(jnp.bfloat16), value_rows, pref...  14 us
    all_to_all x1, waiting for transfers between devices, on_device(): lax.all_to_all(expert_done, 'expert', split_axis=0, concat_axis=0, tiled=...  13.9 us
    while x10, local copies, waits for them, and re-layouts  7.6 us
    slice x2, local copies, waits for them, and re-layouts, add_block(): value_rows = block_rows[:, HD:].reshape(step_len, HEADS, HEAD_DIM)  5.29 us
    gather x1, local copies, waits for them, and re-layouts, on_device(): picked_rows = flat_rows[jnp.maximum(slot_ids, 0)]  4.97 us
  transfers between devices with their start and end apart: 2, of which 2 were waited for; matrix products, arithmetic and copies ran while one was open for 8% of the time, Pallas kernels for 0%

profile of v1, /device:TPU:0, one launch (start us, length us, event | category | flops | bytes accessed | tf_op | source)
XLA Modules:
  0.0 183.1 jit_solution(15243660066245395391)
XLA Ops:
  7.3 2.5 %slice_convert_fusion = (f32[256,1024]{1,0:T(8,128)}, bf16[256,1024]{1,0:T(8,128)(2,1)S(1)}) fusion(bf16[256,2048]{1,0:T(8,128)(2,1)} %param.16), kind=kLoop, calls=%fused_computation.55 | loop fusion | flops 262144 | bytes 2621440 | tf_op jit(solution)/shard_map/convert_element_type | solution.py:86
  10.7 1.2 copy.40
  12.0 2.6 %copy.29 = f32[256,1024]{0,1:T(8,128)} copy(f32[256,1024]{1,0:T(8,128)} %get-tuple-element.119) | data formatting | bytes 2097152 | tf_op jit(solution)/shard_map/convert_element_type | solution.py:86
  19.7 39.1 %all-gather.3.cloned.1.call-done = bf16[1,1024,2048]{2,1,0:T(8,128)(2,1)} async-done(((bf16[1,128,2048]{2,1,0:T(8,128)(2,1)}), bf16[1,1024,2048]{2,1,0:T(8,128)(2,1)}) %all-gather.3.cloned.1.call-update) | async-done | bytes 4194320 | tf_op jit(solution)/shard_map/all_gather | solution.py:88
  58.9 54.3 %while.15 = (s32[]{:T(128)}, f32[16,256]{1,0:T(8,128)}, f32[16,256]{1,0:T(8,128)}, f32[16,256,64]{1,2,0:T(8,128)}, s32[2,512]{1,0:T(2,128)}, /*index=5*/s32[256]...) while((s32[]{:T(128)}, f32[16,256]{1,0:T(8,128)}, ...), condition=%wide.region_5.6_spmd.clone, body=%wide.region_2.5_spmd.clone.sunk | while | flops 560607232 | bytes 76881064 | solution.py:118
  60.4 3.1 %constant_dynamic-slice_fusion.5 = bf16[1,512,2048]{2,1,0:T(8,128)(2,1)} fusion(bf16[2,512,2048]{2,1,0:T(8,128)(2,1)} %get-tuple-element.210, s32[]{:T(128)} %get-tuple-element.194), kind=kLoop, calls=%fused_computation.13.clone.1 | loop fusion | bytes 4194308 | tf_op jit(solution)/shard_map/while/body/jit(dynamic_index_in_dim)/dynamic_slice | solution.py:118
  63.5 3.9 %copy.46 = bf16[1,512,2048]{1,2,0:T(8,128)(2,1)} copy(bf16[1,512,2048]{2,1,0:T(8,128)(2,1)} %constant_dynamic-slice_fusion.5) | data formatting | bytes 4194304 | tf_op jit(solution)/shard_map/while/body/jit(dynamic_index_in_dim)/dynamic_slice | solution.py:118
  67.4 2.6 %fusion.80 = (bf16[512,1024]{0,1:T(8,128)(2,1)}, bf16[512,1024]{0,1:T(8,128)(2,1)S(1)}) fusion(bf16[512,2048]{0,1:T(8,128)(2,1)} %bitcast.102), kind=kLoop, calls=%fused_computation.94.clone.1 | loop fusion | bytes 4194304 | tf_op jit(solution)/shard_map/while/body/eval_jaxpr/slice | solution.py:99
  70.1 1.5 fusion.81
  71.6 3.2 %copy-done.1 = f32[16,512,256]{2,1,0:T(8,128)} copy-done((f32[16,512,256]{2,1,0:T(8,128)}, f32[16,512,256]{2,1,0:T(8,128)S(1)}, u32[]{:S(2)}) %copy-start.1) | copy-done | bytes 8388632 | tf_op jit(solution)/shard_map/while
  74.8 2.3 %fusion.82 = f32[16,256]{1,0:T(8,128)} fusion(f32[16,512,256]{2,1,0:T(8,128)S(1)} %get-tuple-element.180, f32[16,256]{1,0:T(8,128)S(1)} %max.10, pred[256,512]{0,1:T(8,128)(4,1)S(1)} %broadcast_compare_fusion.3), kind=kLoop, calls=%fused_computation.4.clone.1 | loop fusion | flops 8384512 | bytes 8552448 | tf_op jit(solution)/shard_map/while/body/eval_jaxpr/reduce_sum | solution.py:109
  77.1 1.3 fusion.83
  78.4 7.0 %fusion.84 = f32[16,256,64]{1,2,0:T(8,128)} fusion(bf16[512,16,64]{0,2,1:T(8,128)(2,1)} %bitcast.105, f32[16,512,256]{2,1,0:T(8,128)} %copy-done.1, f32[16,256]{1,0:T(8,128)S(1)} %max.10, pred[256,512]{0,1:T(8,128)(4,1)S(1)} %broadcast_compare_fusion.3, f32[16,256,64]{1,2,0:T(8,128)} %get-tuple-element.197, f32[16,256]{1,0:T(8,128)S(1)} %get-tuple-element.183), kind=kOutput, calls=%fused_computation.8.clone.1 | convolution fusion | flops 277348352 | bytes 11698176 | tf_op jit(solution)/shard_map/while/body/eval_jaxpr/hrk,khd->hrd/dot_general | solution.py:110
  87.5 3.1 %constant_dynamic-slice_fusion.5 = bf16[1,512,2048]{2,1,0:T(8,128)(2,1)} fusion(bf16[2,512,2048]{2,1,0:T(8,128)(2,1)} %get-tuple-element.210, s32[]{:T(128)} %get-tuple-element.194), kind=kLoop, calls=%fused_computation.13.clone.1 | loop fusion | bytes 4194308 | tf_op jit(solution)/shard_map/while/body/jit(dynamic_index_in_dim)/dynamic_slice | solution.py:118
  90.7 3.9 %copy.46 = bf16[1,512,2048]{1,2,0:T(8,128)(2,1)} copy(bf16[1,512,2048]{2,1,0:T(8,128)(2,1)} %constant_dynamic-slice_fusion.5) | data formatting | bytes 4194304 | tf_op jit(solution)/shard_map/while/body/jit(dynamic_index_in_dim)/dynamic_slice | solution.py:118
  94.6 2.6 %fusion.80 = (bf16[512,1024]{0,1:T(8,128)(2,1)}, bf16[512,1024]{0,1:T(8,128)(2,1)S(1)}) fusion(bf16[512,2048]{0,1:T(8,128)(2,1)} %bitcast.102), kind=kLoop, calls=%fused_computation.94.clone.1 | loop fusion | bytes 4194304 | tf_op jit(solution)/shard_map/while/body/eval_jaxpr/slice | solution.py:99
  97.2 1.5 fusion.81
  98.8 3.2 %copy-done.1 = f32[16,512,256]{2,1,0:T(8,128)} copy-done((f32[16,512,256]{2,1,0:T(8,128)}, f32[16,512,256]{2,1,0:T(8,128)S(1)}, u32[]{:S(2)}) %copy-start.1) | copy-done | bytes 8388632 | tf_op jit(solution)/shard_map/while
  102.0 2.3 %fusion.82 = f32[16,256]{1,0:T(8,128)} fusion(f32[16,512,256]{2,1,0:T(8,128)S(1)} %get-tuple-element.180, f32[16,256]{1,0:T(8,128)S(1)} %max.10, pred[256,512]{0,1:T(8,128)(4,1)S(1)} %broadcast_compare_fusion.3), kind=kLoop, calls=%fused_computation.4.clone.1 | loop fusion | flops 8384512 | bytes 8552448 | tf_op jit(solution)/shard_map/while/body/eval_jaxpr/reduce_sum | solution.py:109
  104.2 1.4 fusion.83
  105.6 7.0 %fusion.84 = f32[16,256,64]{1,2,0:T(8,128)} fusion(bf16[512,16,64]{0,2,1:T(8,128)(2,1)} %bitcast.105, f32[16,512,256]{2,1,0:T(8,128)} %copy-done.1, f32[16,256]{1,0:T(8,128)S(1)} %max.10, pred[256,512]{0,1:T(8,128)(4,1)S(1)} %broadcast_compare_fusion.3, f32[16,256,64]{1,2,0:T(8,128)} %get-tuple-element.197, f32[16,256]{1,0:T(8,128)S(1)} %get-tuple-element.183), kind=kOutput, calls=%fused_computation.8.clone.1 | convolution fusion | flops 277348352 | bytes 11698176 | tf_op jit(solution)/shard_map/while/body/eval_jaxpr/hrk,khd->hrd/dot_general | solution.py:110
  113.2 1.5 divide_convert_fusion
  114.7 2.7 %multiply_reduce_fusion.1 = (f32[256]{0:T(256)S(1)}, f32[256,1024]{1,0:T(8,128)S(1)}) fusion(bf16[256,1024]{0,1:T(8,128)(2,1)S(1)} %bitcast.110, bf16[1024,1024]{1,0:T(8,128)(2,1)} %param.22, bf16[256,1024]{1,0:T(8,128)(2,1)} %param.21), kind=kOutput, calls=%fused_computation.51 | convolution fusion | flops 537919232 | bytes 4195328 | tf_op jit(solution)/shard_map/dot_general | solution.py:126
  119.0 20.6 %all_to_all.10 = bf16[4,160,1024]{2,1,0:T(8,128)(2,1)S(1)} all-to-all(bf16[4,160,1024]{2,1,0:T(8,128)(2,1)S(1)} %bitcast.107), channel_id=1, replica_groups=mesh['expert'=4,'req'=8] {'expert'}, dimensions={0} | all-to-all | bytes 2621440 | tf_op jit(solution)/shard_map/all_to_all | solution.py:146
  139.6 3.9 %fusion.14 = f32[4,1,160,2816]{3,2,0,1:T(8,128)S(1)} fusion(bf16[4,160,1024]{2,1,0:T(8,128)(2,1)S(1)} %all_to_all.10, bf16[1,1024,2816]{2,1,0:T(8,128)(2,1)S(1)} %bitcast.116), kind=kOutput, calls=%fused_computation.20 | convolution fusion | flops 3690987520 | bytes 14286848 | tf_op jit(solution)/shard_map/slnd,ldf->slnf/dot_general | solution.py:151
  143.5 3.6 %fusion.34 = bf16[4,160,1024]{2,1,0:T(8,128)(2,1)} fusion(bf16[1,1408,1024]{2,1,0:T(8,128)(2,1)S(1)} %copy-done, f32[4,1,160,2816]{3,2,0,1:T(8,128)S(1)} %fusion.14), kind=kOutput, calls=%fused_computation.39 | convolution fusion | flops 1855160320 | bytes 11403264 | tf_op jit(solution)/shard_map/slnf,lfd->slnd/dot_general | solution.py:155
  147.2 4.4 %all-to-all-start.1 = ((bf16[4,160,1024]{2,1,0:T(8,128)(2,1)}), bf16[4,160,1024]{2,1,0:T(8,128)(2,1)}, u32[]{:S(2)}, u32[]{:S(2)}) async-start(bf16[4,160,1024]{2,1,0:T(8,128)(2,1)} %fusion.34), calls=%async_computation.1 | async-start | bytes 2621440 | tf_op jit(solution)/shard_map/all_to_all | solution.py:159
  151.7 1.5 fusion.56
  153.4 13.9 %all-to-all-done.1 = bf16[4,160,1024]{2,1,0:T(8,128)(2,1)} async-done(((bf16[4,160,1024]{2,1,0:T(8,128)(2,1)}), bf16[4,160,1024]{2,1,0:T(8,128)(2,1)}, u32[]{:S(2)}, u32[]{:S(2)}) %all-to-all-start.1) | async-done | bytes 1310752 | tf_op jit(solution)/shard_map/all_to_all | solution.py:159
  167.3 5.0 %gather_fusion = bf16[512,1024]{1,0:T(8,128)(2,1)} fusion(bf16[640,1024]{1,0:T(8,128)(2,1)} %bitcast.25, s32[1024]{0:T(1024)S(1)} %pad_clamp_fusion), kind=kCustom, calls=%fused_computation | custom fusion | bytes 2099200 | tf_op jit(solution)/shard_map/gather | solution.py:161
  172.3 1.6 fusion.28
  173.8 1.4 multiply_reduce_fusion
  (73 shorter events, 13.8 us)
Async XLA Ops:
  6.5 137.0 %copy-start = (bf16[1,1408,1024]{2,1,0:T(8,128)(2,1)S(1)}, bf16[1,1408,1024]{2,1,0:T(8,128)(2,1)}, u32[]{:S(2)}) copy-start(bf16[1,1408,1024]{2,1,0:T(8,128)(2,1)} %param.26) | copy-start | bytes 8650756
  6.5 8.1 %copy-start.14 = (s32[1,8]{1,0:T(1,128)S(1)}, s32[1,8]{1,0:T(1,128)}, u32[]{:S(2)}) copy-start(s32[1,8]{1,0:T(1,128)} %param.18) | copy-start | bytes 100
  6.5 8.3 %copy-start.12 = (bf16[1024]{0:T(1024)(128)(2,1)S(1)}, bf16[1024]{0:T(1024)(128)(2,1)}, u32[]{:S(2)}) copy-start(bf16[1024]{0:T(1024)(128)(2,1)} %param.23) | copy-start | bytes 6148
  6.5 8.8 %copy-start.6 = (s32[256,2]{0,1:T(2,128)S(1)}, s32[256,2]{0,1:T(2,128)}, u32[]{:S(2)}) copy-start(s32[256,2]{0,1:T(2,128)} %param.20) | copy-start | bytes 6148
  6.5 52.3 %all-gather.3.cloned.1.call-start = ((), (), s32[]{:S(2)}) async-start(), calls=%async_computation.2 | async-start | bytes 4718592 | tf_op jit(solution)/shard_map/all_gather | solution.py:88
  15.7 43.2 %copy-start.8 = (s32[2,256]{1,0:T(2,128)}, s32[2,256]{1,0:T(2,128)S(1)}, u32[]{:S(2)}) copy-start(s32[2,256]{1,0:T(2,128)S(1)} %reshape.127) | copy-start | bytes 6148
  70.1 1.5 copy-start.3
  71.6 3.2 %copy-start.1 = (f32[16,512,256]{2,1,0:T(8,128)}, f32[16,512,256]{2,1,0:T(8,128)S(1)}, u32[]{:S(2)}) copy-start(f32[16,512,256]{2,1,0:T(8,128)S(1)} %get-tuple-element.180) | copy-start | bytes 25165828 | tf_op jit(solution)/shard_map/while
  97.2 1.5 copy-start.3
  98.7 3.2 %copy-start.1 = (f32[16,512,256]{2,1,0:T(8,128)}, f32[16,512,256]{2,1,0:T(8,128)S(1)}, u32[]{:S(2)}) copy-start(f32[16,512,256]{2,1,0:T(8,128)S(1)} %get-tuple-element.180) | copy-start | bytes 25165828 | tf_op jit(solution)/shard_map/while
  113.2 5.2 %copy-start.4 = (bf16[640,256]{1,0:T(8,128)(2,1)S(1)}, bf16[640,256]{1,0:T(8,128)(2,1)}, u32[]{:S(2)}) copy-start(bf16[640,256]{1,0:T(8,128)(2,1)} %fusion.43) | copy-start | bytes 983044
  113.2 5.2 %copy-start.5 = (f32[1024]{0:T(1024)S(1)}, f32[1024]{0:T(1024)}, u32[]{:S(2)}) copy-start(f32[1024]{0:T(1024)} %convert_element_type.81) | copy-start | bytes 12292
  113.2 26.4 %slice-start = ((s8[5767168]{0:T(1024)(128)(4,1)}), s8[4194304]{0:T(1024)(128)(4,1)S(1)}, s32[]{:S(2)}) async-start(s8[5767168]{0:T(1024)(128)(4,1)} %bitcast.115), calls=%async_computation.3 | async-start | bytes 8388608
  114.7 24.9 %slice-start.1 = ((s8[5767168]{0:T(1024)(128)(4,1)}), s8[1572864]{0:T(1024)(128)(4,1)S(1)}, s32[]{:S(2)}) async-start(s8[5767168]{0:T(1024)(128)(4,1)} %bitcast.115), calls=%async_computation.4 | async-start | bytes 3145728
  117.4 1.0 copy-start.2
  143.5 8.1 %copy-start.11 = (s32[1,2,2,128]{3,2,1,0:T(2,128)S(1)}, s32[1,2,2,128]{3,2,1,0:T(2,128)}, u32[]{:S(2)}) copy-start(s32[1,2,2,128]{3,2,1,0:T(2,128)} %get-tuple-element.113) | copy-start | bytes 6148
  143.5 8.1 %copy-start.13 = (bf16[1024]{0:T(1024)(128)(2,1)S(1)}, bf16[1024]{0:T(1024)(128)(2,1)}, u32[]{:S(2)}) copy-start(bf16[1024]{0:T(1024)(128)(2,1)} %param.27) | copy-start | bytes 6148
  143.5 8.1 %copy-start.10 = (bf16[1024,4]{0,1:T(4,128)(2,1)S(1)}, bf16[1024,4]{0,1:T(4,128)(2,1)}, u32[]{:S(2)}) copy-start(bf16[1024,4]{0,1:T(4,128)(2,1)} %param.24) | copy-start | bytes 24580
  147.2 6.0 %copy-start.7 = (s32[256,2]{0,1:T(2,128)S(1)}, s32[256,2]{0,1:T(2,128)}, u32[]{:S(2)}) copy-start(s32[256,2]{0,1:T(2,128)} %param.20) | copy-start | bytes 6148
  147.2 6.1 %copy-start.9 = (s32[2,256]{1,0:T(2,128)S(1)}, s32[2,256]{1,0:T(2,128)}, u32[]{:S(2)}) copy-start(s32[2,256]{1,0:T(2,128)} %copy-done.8) | copy-start | bytes 6148
  147.2 20.1 %all-to-all-start.1 = ((bf16[4,160,1024]{2,1,0:T(8,128)(2,1)}), bf16[4,160,1024]{2,1,0:T(8,128)(2,1)}, u32[]{:S(2)}, u32[]{:S(2)}) async-start(bf16[4,160,1024]{2,1,0:T(8,128)(2,1)} %fusion.34), calls=%async_computation.1 | async-start | bytes 2621440 | tf_op jit(solution)/shard_map/all_to_all | solution.py:159
Sparse Core Ops, SparseCore 0:
  9.0 49.8 all-gather.2

commit v2 on v0

v2 whole, which is shorter than its diff:
```python
import functools
import math

import jax
import jax.numpy as jnp
from jax import lax
from jax.experimental import pallas as pl
from jax.experimental.pallas import tpu as pltpu
from jax.sharding import PartitionSpec as P

HEADS = 16
HEAD_DIM = 64
TOP = 2
PAIRS = HEADS // 2
LANES = 2 * HEAD_DIM
HD = HEADS * HEAD_DIM
CORES = 2
HALVES = 2
NORM_EPS = 1e-06
EXP_SCALE = math.log2(math.e) / math.sqrt(HEAD_DIM)
F32 = jnp.float32
BF16 = jnp.bfloat16


def xor_index(a, b, count):
    out, bit = 0, 1
    while bit < count:
        out = out + ((a // bit + b // bit) % 2) * bit
        bit *= 2
    return out


def rms_scale(values, gain_row):
    mean_square = jnp.mean(values * values, axis=-1, keepdims=True)
    return values * lax.rsqrt(mean_square + NORM_EPS) * gain_row


def layer_kernel(
    n_exp,
    n_req,
    q_hbm,
    self_hbm,
    page_hbm,
    table_ref,
    lengths_ref,
    routes_ref,
    routes_t_ref,
    resid_hbm,
    w_attn_hbm,
    gain_attn_ref,
    w_router_ref,
    w_in_hbm,
    w_out_hbm,
    gain_out_ref,
    out_ref,
    kv,
    q,
    self_kv,
    resid_in,
    w_attn,
    w_in,
    w_out,
    bias,
    top,
    acc,
    attended,
    resid,
    normed,
    assign,
    pick,
    gates,
    disp,
    arrived,
    hidden,
    result,
    collected,
    load_sem,
    ring_send,
    pair_send,
    page_recv,
    disp_send,
    disp_recv,
    back_send,
    back_recv,
):
    me_exp = lax.axis_index("expert")
    me_req = lax.axis_index("req")
    z, core = me_req // CORES, me_req % CORES
    n_z = n_req // CORES
    rows = q.shape[0]
    page_len = kv.shape[1]
    half_len = page_len // HALVES
    cap = disp.shape[1]
    hidden_width = w_out.shape[0]
    width = resid.shape[1]
    sibling = z * CORES + (1 - core)

    def at_req(req):
        return {"req": req}

    def at_exp(exp):
        return {"expert": exp}

    loads = [
        (page_hbm.at[0], kv.at[me_req]),
        (q_hbm, q),
        (self_hbm, self_kv),
        (resid_hbm, resid_in),
        (w_attn_hbm, w_attn),
        (w_in_hbm.at[0], w_in),
        (w_out_hbm.at[0], w_out),
    ]
    load = [
        pltpu.make_async_copy(src, dst, load_sem.at[i]) for i, (src, dst) in enumerate(loads)
    ]
    for copy in load:
        copy.start()

    barrier = pltpu.get_barrier_semaphore()

    def greet(device):
        pl.semaphore_signal(
            barrier, inc=1, device_id=device, device_id_type=pl.DeviceIdType.MESH
        )

    greet(at_req(sibling))

    @pl.when(z > 0)
    def _():
        greet(at_req(me_req - CORES))

    @pl.when(z < n_z - 1)
    def _():
        greet(at_req(me_req + CORES))

    for d in range(1, n_exp):
        greet(at_exp(xor_index(me_exp, d, n_exp)))
    pl.semaphore_wait(barrier, n_exp + jnp.where(z > 0, 1, 0) + jnp.where(z < n_z - 1, 1, 0))

    def half_of(page, half):
        return kv.at[page, pl.ds(half * half_len, half_len)]

    def ring_copy(page, half, side, own=False):
        src = page_hbm.at[0, pl.ds(half * half_len, half_len)] if own else half_of(page, half)
        return pltpu.make_async_remote_copy(
            src_ref=src,
            dst_ref=half_of(page, half),
            send_sem=ring_send.at[side, page, half],
            recv_sem=page_recv.at[page, half],
            device_id=at_req(me_req + CORES * (1 - 2 * side)),
            device_id_type=pl.DeviceIdType.MESH,
        )

    def pair_copy(page, half, own=False):
        src = page_hbm.at[0, pl.ds(half * half_len, half_len)] if own else half_of(page, half)
        return pltpu.make_async_remote_copy(
            src_ref=src,
            dst_ref=half_of(page, half),
            send_sem=pair_send.at[page, half],
            recv_sem=page_recv.at[page, half],
            device_id=at_req(sibling),
            device_id_type=pl.DeviceIdType.MESH,
        )

    for half in range(HALVES):

        @pl.when(z < n_z - 1)
        def _():
            ring_copy(me_req, half, 0, own=True).start()

        @pl.when(z > 0)
        def _():
            ring_copy(me_req, half, 1, own=True).start()

    for half in range(HALVES):
        pair_copy(me_req, half, own=True).start()

    strict = (
        lax.broadcasted_iota(jnp.int32, (rows, rows), 0)
        > lax.broadcasted_iota(jnp.int32, (rows, rows), 1)
    ).astype(F32).astype(BF16)
    strict_t = (
        lax.broadcasted_iota(jnp.int32, (rows, rows), 0)
        < lax.broadcasted_iota(jnp.int32, (rows, rows), 1)
    ).astype(F32).astype(BF16)
    exp_lane = lax.broadcasted_iota(jnp.int32, (rows, 128), 1)
    exp_row = lax.broadcasted_iota(jnp.int32, (n_exp, rows), 0)
    total = jnp.zeros((1, 128), F32)
    total_t = jnp.zeros((n_exp, 1), F32)
    slots, slots_t = [], []
    for k in range(TOP):
        route = routes_ref[:, k : k + 1]
        hot = (exp_lane == route).astype(F32)
        before = jnp.dot(strict, hot.astype(BF16), preferred_element_type=F32) + total
        place = jnp.sum(before * hot, axis=1, keepdims=True).astype(jnp.int32)
        slots.append(jnp.where(place < cap, route * cap + place, -1))
        total = total + jnp.sum(hot, axis=0, keepdims=True)
        route_t = routes_t_ref[k : k + 1, :]
        hot_t = (exp_row == route_t).astype(F32)
        before_t = jnp.dot(hot_t.astype(BF16), strict_t, preferred_element_type=F32) + total_t
        place_t = jnp.sum(before_t * hot_t, axis=0, keepdims=True).astype(jnp.int32)
        slots_t.append(jnp.where(place_t < cap, route_t * cap + place_t, -1))
        total_t = total_t + jnp.sum(hot_t, axis=1, keepdims=True)

    def fill_tables(e, carry):
        slot_row = lax.broadcasted_iota(jnp.int32, (cap, rows), 0) + e * cap
        taken = (slot_row == slots_t[0]).astype(F32) + (slot_row == slots_t[1]).astype(F32)
        assign[e] = taken.astype(BF16)
        slot_lane = lax.broadcasted_iota(jnp.int32, (rows, cap), 1) + e * cap
        for k in range(TOP):
            pick[e, k * rows : (k + 1) * rows, :] = (
                (slot_lane == slots[k]).astype(F32).astype(BF16)
            )
        return carry

    lax.fori_loop(0, n_exp, fill_tables, 0)

    first_lanes = lax.broadcasted_iota(jnp.int32, (1, LANES), 1) < HEAD_DIM

    def own_part(pair, carry):
        lanes = pl.ds(pl.multiple_of(pair * LANES, LANES), LANES)
        product = q[:, lanes].astype(F32) * self_kv[:, lanes].astype(F32)
        own_value = self_kv[
            :, pl.ds(pl.multiple_of(HD + pair * LANES, LANES), LANES)
        ].astype(F32)
        for i in range(2):
            mine = first_lanes if i == 0 else jnp.logical_not(first_lanes)
            score = jnp.sum(jnp.where(mine, product, 0.0), axis=1, keepdims=True)
            top[2 * pair + i] = jnp.broadcast_to(score, (rows, LANES))
            acc[2 * pair + i] = jnp.where(mine, own_value, 1.0)
        return carry

    load[1].wait()
    load[2].wait()
    lax.fori_loop(0, PAIRS, own_part, 0)

    keys = CORES * page_len
    table = table_ref[...]
    logical = lax.broadcasted_iota(jnp.int32, table.shape, 1)

    def attend(block_z):
        key_lane = lax.broadcasted_iota(jnp.int32, (1, keys), 1)
        place = key_lane % page_len
        for c in range(CORES):
            at = jnp.sum(
                jnp.where(table == block_z * CORES + c, logical, 0), axis=1, keepdims=True
            )
            place = place + jnp.where(key_lane // page_len == c, at * page_len, 0)
        bias[...] = jnp.where(place < lengths_ref[...], 0.0, -jnp.inf)

        def heads(pair, carry):
            lanes = pl.ds(pl.multiple_of(pair * LANES, LANES), LANES)
            value_lanes = pl.ds(pl.multiple_of(HD + pair * LANES, LANES), LANES)
            query = q[:, lanes]
            key = jnp.concatenate(
                [kv[block_z * CORES + c, :, lanes] for c in range(CORES)], axis=0
            )
            value = jnp.concatenate(
                [kv[block_z * CORES + c, :, value_lanes] for c in range(CORES)], axis=0
            )
            for i in range(2):
                mine = first_lanes if i == 0 else jnp.logical_not(first_lanes)
                score = lax.dot_general(
                    jnp.where(mine, query, jnp.zeros_like(query)),
                    key,
                    (((1,), (1,)), ((), ())),
                    preferred_element_type=F32,
                ) + bias[...]
                old = top[2 * pair + i]
                new = jnp.maximum(old, jnp.max(score, axis=1, keepdims=True))
                weight = jnp.exp2(
                    (score - jnp.concatenate([new] * (keys // LANES), axis=1)) * EXP_SCALE
                )
                factor = jnp.exp2((old - new) * EXP_SCALE)
                top[2 * pair + i] = new
                acc[2 * pair + i] = acc[2 * pair + i] * factor + jnp.dot(
                    weight.astype(BF16),
                    jnp.where(mine, value, jnp.ones_like(value)),
                    preferred_element_type=F32,
                )
            return carry

        def heads_two(step, carry):
            heads(2 * step, carry)
            heads(2 * step + 1, carry)
            return carry

        lax.fori_loop(0, PAIRS // 2, heads_two, 0)

    load[0].wait()
    for half in range(HALVES):
        pair_copy(sibling, half).wait_recv()
    attend(z)

    def stage(s, carry):
        for half in range(HALVES):
            for side in range(2):
                block_z = z - s if side == 0 else z + s
                here = block_z >= 0 if side == 0 else block_z < n_z
                onward = z < n_z - 1 if side == 0 else z > 0
                page = block_z * CORES + core

                @pl.when(here)
                def _():
                    ring_copy(page, half, side).wait_recv()

                    @pl.when(onward)
                    def _():
                        ring_copy(page, half, side).start()

                    pair_copy(page, half).start()

        for side in range(2):
            block_z = z - s if side == 0 else z + s
            here = block_z >= 0 if side == 0 else block_z < n_z

            @pl.when(here)
            def _():
                for half in range(HALVES):
                    pair_copy(block_z * CORES + (1 - core), half).wait_recv()
                attend(block_z)

        return carry

    lax.fori_loop(1, n_z, stage, 0)

    for pair in range(PAIRS):
        first, second = acc[2 * pair], acc[2 * pair + 1]
        attended[:, pair * LANES : (pair + 1) * LANES] = jnp.where(
            first_lanes,
            first / first[:, LANES - 1 : LANES],
            second / second[:, 0:1],
        ).astype(BF16)

    load[3].wait()
    load[4].wait()
    step_cols = 256
    for c in range(0, width, step_cols):
        resid[:, c : c + step_cols] = resid_in[:, c : c + step_cols].astype(F32) + jnp.dot(
            attended[...], w_attn[:, c : c + step_cols], preferred_element_type=F32
        )
    normed[...] = rms_scale(resid[...], gain_attn_ref[...].astype(F32)).astype(BF16)

    def disp_copy(exp, source):
        return pltpu.make_async_remote_copy(
            src_ref=disp.at[exp],
            dst_ref=arrived.at[source],
            send_sem=disp_send.at[exp],
            recv_sem=disp_recv.at[source],
            device_id=at_exp(exp),
            device_id_type=pl.DeviceIdType.MESH,
        )

    def back_copy(source, exp):
        return pltpu.make_async_remote_copy(
            src_ref=result.at[source],
            dst_ref=collected.at[exp],
            send_sem=back_send.at[source],
            recv_sem=back_recv.at[exp],
            device_id=at_exp(source),
            device_id_type=pl.DeviceIdType.MESH,
        )

    def gather_slots(exp):
        return jnp.dot(assign[exp], normed[...], preferred_element_type=F32).astype(BF16)

    def send_slots(d, carry):
        exp = xor_index(me_exp, d, n_exp)
        disp[exp] = gather_slots(exp)
        disp_copy(exp, me_exp).start()
        return carry

    lax.fori_loop(1, n_exp, send_slots, 0)
    arrived[me_exp] = gather_slots(me_exp)

    logits = jnp.dot(normed[...], w_router_ref[...], preferred_element_type=F32)
    router_lane = lax.broadcasted_iota(jnp.int32, logits.shape, 1)
    chosen = [
        jnp.sum(
            jnp.where(router_lane == routes_ref[:, k : k + 1], logits, 0.0),
            axis=1,
            keepdims=True,
        )
        for k in range(TOP)
    ]
    for k in range(TOP):
        gates[k] = jnp.broadcast_to(
            jax.nn.sigmoid(chosen[k] - chosen[1 - k]), (rows, 128)
        )

    load[5].wait()
    load[6].wait()

    def expert(source):
        x = arrived[source]
        for f in range(0, hidden_width, step_cols):
            size = min(step_cols, hidden_width - f)
            gate = jnp.dot(x, w_in[:, f : f + size], preferred_element_type=F32)
            up = jnp.dot(
                x,
                w_in[:, hidden_width + f : hidden_width + f + size],
                preferred_element_type=F32,
            )
            hidden[:, f : f + size] = (jax.nn.gelu(gate, approximate=True) * up).astype(BF16)
        for c in range(0, width, step_cols):
            result[source, :, c : c + step_cols] = jnp.dot(
                hidden[...], w_out[:, c : c + step_cols], preferred_element_type=F32
            ).astype(BF16)

    def serve(d, carry):
        source = xor_index(me_exp, d, n_exp)

        @pl.when(d > 0)
        def _():
            disp_copy(me_exp, source).wait_recv()

        expert(source)

        @pl.when(d > 0)
        def _():
            back_copy(source, me_exp).start()

        return carry

    lax.fori_loop(0, n_exp, serve, 0)

    def combine(exp, rows_of):
        both = jnp.dot(pick[exp], rows_of, preferred_element_type=F32)
        resid[...] += both[:rows] * gates[0, :, 0:1] + both[rows:] * gates[1, :, 0:1]

    combine(me_exp, result[me_exp])

    def take(d, carry):
        exp = xor_index(me_exp, d, n_exp)
        back_copy(me_exp, exp).wait_recv()
        combine(exp, collected[exp])
        return carry

    lax.fori_loop(1, n_exp, take, 0)
    out_ref[...] = rms_scale(resid[...], gain_out_ref[...].astype(F32)).astype(BF16)

    def sent(d, carry):
        other = xor_index(me_exp, d, n_exp)
        disp_copy(other, me_exp).wait_send()
        back_copy(other, me_exp).wait_send()
        return carry

    lax.fori_loop(1, n_exp, sent, 0)

    def pages_sent(s, carry):
        for side in range(2):
            block_z = z - s if side == 0 else z + s
            here = block_z >= 0 if side == 0 else block_z < n_z
            onward = z < n_z - 1 if side == 0 else z > 0
            page = block_z * CORES + core

            @pl.when(here)
            def _():
                for half in range(HALVES):

                    @pl.when(onward)
                    def _():
                        ring_copy(page, half, side).wait_send()

                    pair_copy(page, half).wait_send()

        return carry

    lax.fori_loop(1, n_z, pages_sent, 0)
    for half in range(HALVES):

        @pl.when(z < n_z - 1)
        def _():
            ring_copy(me_req, half, 0, own=True).wait_send()

        @pl.when(z > 0)
        def _():
            ring_copy(me_req, half, 1, own=True).wait_send()

        pair_copy(me_req, half, own=True).wait_send()


def on_device(
    n_exp,
    n_req,
    queries,
    self_kv,
    kv_pages,
    page_table,
    lengths,
    routes,
    residual,
    w_attn_out,
    gain_attn,
    w_router,
    w_in,
    w_out,
    gain_out,
):
    rows, width = residual.shape
    page_len = kv_pages.shape[1]
    hidden_width = w_out.shape[1]
    cap = (5 * rows * TOP + 4 * n_exp - 1) // (4 * n_exp)
    vmem = pl.BlockSpec(memory_space=pltpu.VMEM)
    hbm = pl.BlockSpec(memory_space=pl.ANY)
    dma = pltpu.SemaphoreType.DMA
    return pl.pallas_call(
        functools.partial(layer_kernel, n_exp, n_req),
        out_shape=jax.ShapeDtypeStruct((rows, width), BF16),
        in_specs=[hbm, hbm, hbm, vmem, vmem, vmem, vmem, hbm, hbm, vmem, vmem, hbm, hbm, vmem],
        out_specs=vmem,
        scratch_shapes=[
            pltpu.VMEM((n_req, page_len, 2 * HD), BF16),
            pltpu.VMEM((rows, HD), BF16),
            pltpu.VMEM((rows, 2 * HD), BF16),
            pltpu.VMEM((rows, width), BF16),
            pltpu.VMEM((HD, width), BF16),
            pltpu.VMEM((width, 2 * hidden_width), BF16),
            pltpu.VMEM((hidden_width, width), BF16),
            pltpu.VMEM((rows, CORES * page_len), F32),
            pltpu.VMEM((HEADS, rows, LANES), F32),
            pltpu.VMEM((HEADS, rows, LANES), F32),
            pltpu.VMEM((rows, HD), BF16),
            pltpu.VMEM((rows, width), F32),
            pltpu.VMEM((rows, width), BF16),
            pltpu.VMEM((n_exp, cap, rows), BF16),
            pltpu.VMEM((n_exp, TOP * rows, cap), BF16),
            pltpu.VMEM((TOP, rows, 128), F32),
            pltpu.VMEM((n_exp, cap, width), BF16),
            pltpu.VMEM((n_exp, cap, width), BF16),
            pltpu.VMEM((cap, hidden_width), BF16),
            pltpu.VMEM((n_exp, cap, width), BF16),
            pltpu.VMEM((n_exp, cap, width), BF16),
            dma((7,)),
            dma((2, n_req, HALVES)),
            dma((n_req, HALVES)),
            dma((n_req, HALVES)),
            dma((n_exp,)),
            dma((n_exp,)),
            dma((n_exp,)),
            dma((n_exp,)),
        ],
        compiler_params=pltpu.CompilerParams(
            collective_id=0, has_side_effects=True, vmem_limit_bytes=56 * 2**20
        ),
    )(
        queries,
        self_kv,
        kv_pages,
        page_table,
        lengths.reshape(rows, 1),
        routes,
        routes.T,
        residual,
        w_attn_out,
        gain_attn.reshape(1, width),
        w_router,
        w_in,
        w_out,
        gain_out.reshape(1, width),
    )


def solution(mesh):
    in_specs = (
        P(("expert", "req"), None),
        P(("expert", "req"), None),
        P(("expert", "req"), None, None),
        P("expert", None),
        P(("expert", "req")),
        P(("expert", "req"), None),
        P(("expert", "req"), None),
        P(),
        P(),
        P(),
        P("expert", None, None),
        P("expert", None, None),
        P(),
    )
    out_specs = P(("expert", "req"), None)
    return jax.shard_map(
        functools.partial(on_device, mesh.shape["expert"], mesh.shape["req"]),
        mesh=mesh,
        in_specs=in_specs,
        out_specs=out_specs,
        check_vma=False,
    )
```

time: 184 us -> 90 us (0.49)
  the two profiles are of different devices: /device:TPU:0 before, /device:TPU:30 now
where the time goes in v2:
time: 90 us; the launch traced here: 89.7 us
  Pallas kernels  80.8 us (90%)
  local copies, waits for them, and re-layouts  8.92 us (10%)
    pallas_call x1, Pallas kernels, on_device(): pl.pallas_call(functools.partial(layer_kernel, n_exp, n_req), out_shape=j...  80.8 us
    unnamed x3, local copies, waits for them, and re-layouts  4.9 us

profile of v2, /device:TPU:30, one launch (start us, length us, event | category | flops | bytes accessed | tf_op | source)
XLA Modules:
  0.0 89.7 jit_solution(11190312738057648126)
XLA Ops:
  0.0 1.3 %reshape.10.gain_attn_ref = bf16[1,1024]{1,0:T(2,128)(2,1)} reshape(bf16[1024]{0:T(1024)(128)(2,1)} %param.21) | data formatting | bytes 4096 | tf_op jit(solution)/shard_map/reshape | solution.py:556
  1.3 1.3 %reshape.11.gain_out_ref = bf16[1,1024]{1,0:T(2,128)(2,1)} reshape(bf16[1024]{0:T(1024)(128)(2,1)} %param.25) | data formatting | bytes 4096 | tf_op jit(solution)/shard_map/reshape | solution.py:560
  2.5 1.5 %copy.16.lengths_ref = s32[256,1]{1,0:T(8,128)} copy(s32[256,1]{0,1:T(1,128)} %bitcast.3) | data formatting | bytes 2048 | tf_op jit(solution)/shard_map/reshape | solution.py:551
  4.0 1.5 %copy.17.routes_ref = s32[256,2]{1,0:T(8,128)} copy(s32[256,2]{0,1:T(2,128)} %param.18) | data formatting | bytes 4096 | tf_op args[5]
  5.5 1.6 %copy.18.w_router_ref = bf16[1024,4]{1,0:T(8,128)(2,1)} copy(bf16[1024,4]{0,1:T(4,128)(2,1)} %param.22) | data formatting | bytes 16384 | tf_op args[9]
  7.0 80.8 %shard_map.127 = bf16[256,1024]{1,0:T(8,128)(2,1)} custom-call(bf16[256,1024]{1,0:T(8,128)(2,1)} %q_hbm.1, bf16[256,2048]{1,0:T(8,128)(2,1)} %self_hbm.1, bf16[1,128,2048]{2,1,0:T(8,128)(2,1)} %page_hbm.1, s32[1,8]{1,0:T(1,128)} %table_ref.1, s32[256,1]{1,0:T(8,128)} %copy.16.lengths_ref, s32[256,2]{1,0:T(8,128)} %copy.17.routes_ref, s32[2,256]{1,0:T(2,128)} %bitcast.2, ...), custom_call_target="tpu_custom_call" | custom-call | tf_op jit(solution)/shard_map/pallas_call | solution.py:507
  87.8 1.9 %copy.20 = bf16[256,1024]{1,0:T(8,128)(2,1)} copy(bf16[256,1024]{1,0:T(8,128)(2,1)} %shard_map.127) | data formatting | bytes 1048576

commit v3 on v2

--- a/solution.py
+++ b/solution.py
@@ -35,6 +35,11 @@
     return values * lax.rsqrt(mean_square + NORM_EPS) * gain_row
 
 
+def gain_row(gain_ref):
+    gain = gain_ref[...].astype(F32)
+    return jnp.concatenate([gain[i : i + 1, :] for i in range(gain.shape[0])], axis=1)
+
+
 def layer_kernel(
     n_exp,
     n_req,
@@ -42,13 +47,12 @@
     self_hbm,
     page_hbm,
     table_ref,
-    lengths_ref,
-    routes_ref,
+    lengths_t_ref,
     routes_t_ref,
     resid_hbm,
     w_attn_hbm,
     gain_attn_ref,
-    w_router_ref,
+    w_router_t_ref,
     w_in_hbm,
     w_out_hbm,
     gain_out_ref,
@@ -175,6 +179,15 @@
     for half in range(HALVES):
         pair_copy(me_req, half, own=True).start()
 
+    diagonal = lax.broadcasted_iota(jnp.int32, (rows, rows), 0) == lax.broadcasted_iota(
+        jnp.int32, (rows, rows), 1
+    )
+
+    def to_column(row):
+        return jnp.sum(jnp.where(diagonal, row, 0), axis=1, keepdims=True)
+
+    lengths = to_column(lengths_t_ref[...])
+    routes = [to_column(routes_t_ref[k : k + 1, :]) for k in range(TOP)]
     strict = (
         lax.broadcasted_iota(jnp.int32, (rows, rows), 0)
         > lax.broadcasted_iota(jnp.int32, (rows, rows), 1)
@@ -189,7 +202,7 @@
     total_t = jnp.zeros((n_exp, 1), F32)
     slots, slots_t = [], []
     for k in range(TOP):
-        route = routes_ref[:, k : k + 1]
+        route = routes[k]
         hot = (exp_lane == route).astype(F32)
         before = jnp.dot(strict, hot.astype(BF16), preferred_element_type=F32) + total
         place = jnp.sum(before * hot, axis=1, keepdims=True).astype(jnp.int32)
@@ -246,7 +259,7 @@
                 jnp.where(table == block_z * CORES + c, logical, 0), axis=1, keepdims=True
             )
             place = place + jnp.where(key_lane // page_len == c, at * page_len, 0)
-        bias[...] = jnp.where(place < lengths_ref[...], 0.0, -jnp.inf)
+        bias[...] = jnp.where(place < lengths, 0.0, -jnp.inf)
 
         def heads(pair, carry):
             lanes = pl.ds(pl.multiple_of(pair * LANES, LANES), LANES)
@@ -310,19 +323,18 @@
 
                     pair_copy(page, half).start()
 
-        for side in range(2):
-            block_z = z - s if side == 0 else z + s
-            here = block_z >= 0 if side == 0 else block_z < n_z
-
-            @pl.when(here)
+            before_z = z - s + 1 if half == 0 else z + s - 1
+            before = before_z >= 0 if half == 0 else before_z < n_z
+
+            @pl.when(jnp.logical_and(before, s > 1))
             def _():
-                for half in range(HALVES):
-                    pair_copy(block_z * CORES + (1 - core), half).wait_recv()
-                attend(block_z)
-
-        return carry
-
-    lax.fori_loop(1, n_z, stage, 0)
+                for part in range(HALVES):
+                    pair_copy(before_z * CORES + (1 - core), part).wait_recv()
+                attend(before_z)
+
+        return carry
+
+    lax.fori_loop(1, n_z + 1, stage, 0)
 
     for pair in range(PAIRS):
         first, second = acc[2 * pair], acc[2 * pair + 1]
@@ -339,7 +351,7 @@
         resid[:, c : c + step_cols] = resid_in[:, c : c + step_cols].astype(F32) + jnp.dot(
             attended[...], w_attn[:, c : c + step_cols], preferred_element_type=F32
         )
-    normed[...] = rms_scale(resid[...], gain_attn_ref[...].astype(F32)).astype(BF16)
+    normed[...] = rms_scale(resid[...], gain_row(gain_attn_ref)).astype(BF16)
 
     def disp_copy(exp, source):
         return pltpu.make_async_remote_copy(
@@ -373,11 +385,16 @@
     lax.fori_loop(1, n_exp, send_slots, 0)
     arrived[me_exp] = gather_slots(me_exp)
 
-    logits = jnp.dot(normed[...], w_router_ref[...], preferred_element_type=F32)
+    logits = lax.dot_general(
+        normed[...],
+        w_router_t_ref[...],
+        (((1,), (1,)), ((), ())),
+        preferred_element_type=F32,
+    )
     router_lane = lax.broadcasted_iota(jnp.int32, logits.shape, 1)
     chosen = [
         jnp.sum(
-            jnp.where(router_lane == routes_ref[:, k : k + 1], logits, 0.0),
+            jnp.where(router_lane == routes[k], logits, 0.0),
             axis=1,
             keepdims=True,
         )
@@ -437,7 +454,7 @@
         return carry
 
     lax.fori_loop(1, n_exp, take, 0)
-    out_ref[...] = rms_scale(resid[...], gain_out_ref[...].astype(F32)).astype(BF16)
+    out_ref[...] = rms_scale(resid[...], gain_row(gain_out_ref)).astype(BF16)
 
     def sent(d, carry):
         other = xor_index(me_exp, d, n_exp)
@@ -507,7 +524,7 @@
     return pl.pallas_call(
         functools.partial(layer_kernel, n_exp, n_req),
         out_shape=jax.ShapeDtypeStruct((rows, width), BF16),
-        in_specs=[hbm, hbm, hbm, vmem, vmem, vmem, vmem, hbm, hbm, vmem, vmem, hbm, hbm, vmem],
+        in_specs=[hbm, hbm, hbm, vmem, vmem, vmem, hbm, hbm, vmem, vmem, hbm, hbm, vmem],
         out_specs=vmem,
         scratch_shapes=[
             pltpu.VMEM((n_req, page_len, 2 * HD), BF16),
@@ -548,16 +565,15 @@
         self_kv,
         kv_pages,
         page_table,
-        lengths.reshape(rows, 1),
-        routes,
+        lengths.reshape(1, rows),
         routes.T,
         residual,
         w_attn_out,
-        gain_attn.reshape(1, width),
-        w_router,
+        gain_attn.reshape(width // 128, 128),
+        w_router.T,
         w_in,
         w_out,
-        gain_out.reshape(1, width),
+        gain_out.reshape(width // 128, 128),
     )
 
 

time: 90 us -> 83.3 us (0.926)
  the two profiles are of different devices: /device:TPU:30 before, /device:TPU:0 now
where the time goes in v3:
time: 83.3 us; the launch traced here: 83.1 us
  Pallas kernels  81.2 us (97%)
  local copies, waits for them, and re-layouts  1.87 us (2%)
    pallas_call x1, Pallas kernels, on_device(): pl.pallas_call(functools.partial(layer_kernel, n_exp, n_req), out_shape=j...  81.2 us
    unnamed x1, local copies, waits for them, and re-layouts  1.87 us

profile of v3, /device:TPU:0, one launch (start us, length us, event | category | flops | bytes accessed | tf_op | source)
XLA Modules:
  0.0 83.1 jit_solution(2753547341525900848)
XLA Ops:
  0.0 81.2 %shard_map.127 = bf16[256,1024]{1,0:T(8,128)(2,1)} custom-call(bf16[256,1024]{1,0:T(8,128)(2,1)} %q_hbm.1, bf16[256,2048]{1,0:T(8,128)(2,1)} %self_hbm.1, bf16[1,128,2048]{2,1,0:T(8,128)(2,1)} %page_hbm.1, s32[1,8]{1,0:T(1,128)} %table_ref.1, s32[1,256]{1,0:T(1,128)} %bitcast.9, s32[2,256]{1,0:T(2,128)} %bitcast.6, bf16[256,1024]{1,0:T(8,128)(2,1)} %resid_hbm.1, ...), custom_call_target="tpu_custom_call" | custom-call | tf_op jit(solution)/shard_map/pallas_call | solution.py:524
  81.2 1.9 %copy.15 = bf16[256,1024]{1,0:T(8,128)(2,1)} copy(bf16[256,1024]{1,0:T(8,128)(2,1)} %shard_map.127) | data formatting | bytes 1048576

commit v4 on v3

--- a/solution.py
+++ b/solution.py
@@ -142,7 +142,7 @@
     pl.semaphore_wait(barrier, n_exp + jnp.where(z > 0, 1, 0) + jnp.where(z < n_z - 1, 1, 0))
 
     def half_of(page, half):
-        return kv.at[page, pl.ds(half * half_len, half_len)]
+        return kv.at[page, pl.ds(pl.multiple_of(half * half_len, half_len), half_len)]
 
     def ring_copy(page, half, side, own=False):
         src = page_hbm.at[0, pl.ds(half * half_len, half_len)] if own else half_of(page, half)
@@ -247,18 +247,19 @@
     load[2].wait()
     lax.fori_loop(0, PAIRS, own_part, 0)
 
-    keys = CORES * page_len
+    keys = CORES * half_len
     table = table_ref[...]
     logical = lax.broadcasted_iota(jnp.int32, table.shape, 1)
 
-    def attend(block_z):
+    def attend(block_z, half):
+        span = pl.ds(pl.multiple_of(half * half_len, half_len), half_len)
         key_lane = lax.broadcasted_iota(jnp.int32, (1, keys), 1)
-        place = key_lane % page_len
+        place = key_lane % half_len + half * half_len
         for c in range(CORES):
             at = jnp.sum(
                 jnp.where(table == block_z * CORES + c, logical, 0), axis=1, keepdims=True
             )
-            place = place + jnp.where(key_lane // page_len == c, at * page_len, 0)
+            place = place + jnp.where(key_lane // half_len == c, at * page_len, 0)
         bias[...] = jnp.where(place < lengths, 0.0, -jnp.inf)
 
         def heads(pair, carry):
@@ -266,10 +267,10 @@
             value_lanes = pl.ds(pl.multiple_of(HD + pair * LANES, LANES), LANES)
             query = q[:, lanes]
             key = jnp.concatenate(
-                [kv[block_z * CORES + c, :, lanes] for c in range(CORES)], axis=0
+                [kv[block_z * CORES + c, span, lanes] for c in range(CORES)], axis=0
             )
             value = jnp.concatenate(
-                [kv[block_z * CORES + c, :, value_lanes] for c in range(CORES)], axis=0
+                [kv[block_z * CORES + c, span, value_lanes] for c in range(CORES)], axis=0
             )
             for i in range(2):
                 mine = first_lanes if i == 0 else jnp.logical_not(first_lanes)
@@ -303,38 +304,38 @@
     load[0].wait()
     for half in range(HALVES):
         pair_copy(sibling, half).wait_recv()
-    attend(z)
-
-    def stage(s, carry):
-        for half in range(HALVES):
-            for side in range(2):
-                block_z = z - s if side == 0 else z + s
-                here = block_z >= 0 if side == 0 else block_z < n_z
-                onward = z < n_z - 1 if side == 0 else z > 0
-                page = block_z * CORES + core
-
-                @pl.when(here)
+        attend(z, half)
+
+    def stage(t, carry):
+        s, half = t // HALVES + 1, t % HALVES
+        for side in range(2):
+            block_z = z - s if side == 0 else z + s
+            here = block_z >= 0 if side == 0 else block_z < n_z
+            onward = z < n_z - 1 if side == 0 else z > 0
+            page = block_z * CORES + core
+
+            @pl.when(here)
+            def _():
+                ring_copy(page, half, side).wait_recv()
+
+                @pl.when(onward)
                 def _():
-                    ring_copy(page, half, side).wait_recv()
-
-                    @pl.when(onward)
-                    def _():
-                        ring_copy(page, half, side).start()
-
-                    pair_copy(page, half).start()
-
-            before_z = z - s + 1 if half == 0 else z + s - 1
-            before = before_z >= 0 if half == 0 else before_z < n_z
-
-            @pl.when(jnp.logical_and(before, s > 1))
+                    ring_copy(page, half, side).start()
+
+                pair_copy(page, half).start()
+
+        for side in range(2):
+            block_z = z - s if side == 0 else z + s
+            here = block_z >= 0 if side == 0 else block_z < n_z
+
+            @pl.when(here)
             def _():
-                for part in range(HALVES):
-                    pair_copy(before_z * CORES + (1 - core), part).wait_recv()
-                attend(before_z)
-
-        return carry
-
-    lax.fori_loop(1, n_z + 1, stage, 0)
+                pair_copy(block_z * CORES + (1 - core), half).wait_recv()
+                attend(block_z, half)
+
+        return carry
+
+    lax.fori_loop(0, HALVES * (n_z - 1), stage, 0)
 
     for pair in range(PAIRS):
         first, second = acc[2 * pair], acc[2 * pair + 1]
@@ -534,7 +535,7 @@
             pltpu.VMEM((HD, width), BF16),
             pltpu.VMEM((width, 2 * hidden_width), BF16),
             pltpu.VMEM((hidden_width, width), BF16),
-            pltpu.VMEM((rows, CORES * page_len), F32),
+            pltpu.VMEM((rows, CORES * page_len // HALVES), F32),
             pltpu.VMEM((HEADS, rows, LANES), F32),
             pltpu.VMEM((HEADS, rows, LANES), F32),
             pltpu.VMEM((rows, HD), BF16),

time: 83.3 us -> 81.1 us (0.974)
  Pallas kernels: 81.2 us -> 79 us
    pallas_call x1, Pallas kernels: 81.2 us -> 79 us  [on_device(): pl.pallas_call(functools.partial(layer_kernel, n_exp, n_req), out_shape=j...]
where the time goes in v4:
time: 81.1 us; the launch traced here: 80.9 us
  Pallas kernels  79 us (97%)
  local copies, waits for them, and re-layouts  1.87 us (2%)
    pallas_call x1, Pallas kernels, on_device(): pl.pallas_call(functools.partial(layer_kernel, n_exp, n_req), out_shape=j...  79 us
    unnamed x1, local copies, waits for them, and re-layouts  1.87 us

profile of v4, /device:TPU:0, one launch (start us, length us, event | category | flops | bytes accessed | tf_op | source)
XLA Modules:
  0.0 80.9 jit_solution(13696651082388365823)
XLA Ops:
  0.0 79.0 %shard_map.127 = bf16[256,1024]{1,0:T(8,128)(2,1)} custom-call(bf16[256,1024]{1,0:T(8,128)(2,1)} %q_hbm.1, bf16[256,2048]{1,0:T(8,128)(2,1)} %self_hbm.1, bf16[1,128,2048]{2,1,0:T(8,128)(2,1)} %page_hbm.1, s32[1,8]{1,0:T(1,128)} %table_ref.1, s32[1,256]{1,0:T(1,128)} %bitcast.9, s32[2,256]{1,0:T(2,128)} %bitcast.6, bf16[256,1024]{1,0:T(8,128)(2,1)} %resid_hbm.1, ...), custom_call_target="tpu_custom_call" | custom-call | tf_op jit(solution)/shard_map/pallas_call | solution.py:525
  79.0 1.9 %copy.15 = bf16[256,1024]{1,0:T(8,128)(2,1)} copy(bf16[256,1024]{1,0:T(8,128)(2,1)} %shard_map.127) | data formatting | bytes 1048576
